TPU v7x, 512 devices: a whole 4x8x8 slice. The times are simulated.
512 devices in a mesh: ctx: 64 (over y_lo, z, core), head: 8 (over y_hi, x).
Axes of the slice: x: 4, y: 8 (y_hi: 2, y_lo: 4; y = y_hi * 4 + y_lo), z: 8, core: 2. Of those that a mesh axis runs over, the one named last changes fastest.
Arguments:
- queries: bfloat16 [32, 65536, 128], P('head', 'ctx'), may hold values from -8 to 8
- cache_keys: bfloat16 [8, 131072, 128], P('head', 'ctx'), may hold values from -8 to 8
- cache_values: bfloat16 [8, 131072, 128], P('head', 'ctx'), may hold values from -8 to 8
- stretch_keys: bfloat16 [8, 65536, 128], P('head', 'ctx'), may hold values from -8 to 8
- stretch_values: bfloat16 [8, 65536, 128], P('head', 'ctx'), may hold values from -8 to 8
- verticals: int32 [8, 8], P('head'), may hold values from 0 to 1023, as said below
- slashes: int32 [8, 4], P('head'), may hold values from 1 to 32, as said below
Outputs:
- attended: bfloat16 [32, 65536, 128], P('head', 'ctx')
Inputs may be any that keep to these rules, and one draw needn't show every extreme that they name: `verticals`: each row names 8 different blocks; block 0 and the last block of the prefix are in every row, and 2 of a row's blocks lie below 16. `slashes`: entry i of a row (i = 1 to 4) lies above (i - 1) * 8 and at most at i * 8; the last entry equals 32.
All inputs are finite; a program needn't handle non-finite values.
Results may differ from a plain program's by a relative error of at most 0.0049.
Values may be sent and summed in bfloat16 or wider, within the bound.
A program may use at most 64 MiB of HBM per device.

v0:
```python
import math

import jax
import jax.numpy as jnp
from jax import lax
from jax.sharding import PartitionSpec as P

BLK = 128
SPAN = 4


def passed_along(x, axis, by):
    peers = lax.axis_size(axis)
    pairs = [(i, i + by) for i in range(peers) if 0 <= i + by < peers]
    return lax.ppermute(x, axis, pairs)


def attend_group(
    query_heads, remote_keys, remote_values, adjacent_keys, adjacent_values, allowed, logit_scale
):
    block_count = adjacent_keys.shape[0]

    def one_head(query_matrix):
        row_count = query_matrix.shape[0]
        distant_scores = (
            jnp.einsum("qd,kd->qk", query_matrix, remote_keys, preferred_element_type=jnp.float32)
            * logit_scale
        )
        distant_scores = distant_scores.reshape(block_count, BLK, -1)
        blocked_mask = query_matrix.reshape(block_count, BLK, -1)
        nearby_scores = (
            jnp.einsum(
                "ohx,ojx->ohj", blocked_mask, adjacent_keys, preferred_element_type=jnp.float32
            )
            * logit_scale
        )
        nearby_scores = jnp.where(allowed, nearby_scores, -jnp.inf)
        highest = jnp.maximum(jnp.max(distant_scores, axis=-1), jnp.max(nearby_scores, axis=-1))[
            ..., None
        ]
        distant_exp = jnp.exp(distant_scores - highest)
        nearby_exp = jnp.exp(nearby_scores - highest)
        row_sum = jnp.sum(distant_exp, axis=-1, keepdims=True) + jnp.sum(
            nearby_exp, axis=-1, keepdims=True
        )
        distant_weight = (distant_exp / row_sum).astype(jnp.bfloat16)
        nearby_weight = (nearby_exp / row_sum).astype(jnp.bfloat16)
        attention_output = jnp.einsum(
            "out,tv->ouv", distant_weight, remote_values, preferred_element_type=jnp.float32
        )
        attention_output = attention_output + jnp.einsum(
            "pnt,ptc->pnc", nearby_weight, adjacent_values, preferred_element_type=jnp.float32
        )
        return attention_output.reshape(row_count, -1).astype(jnp.bfloat16)

    return lax.map(one_head, query_heads)


def local(queries, cache_keys, cache_values, stretch_keys, stretch_values, verticals, slashes):
    kv_here = cache_keys.shape[0]
    query_rows = queries.shape[1]
    head_dim = queries.shape[2]
    query_blocks = query_rows // BLK
    cache_blocks = cache_keys.shape[1] // BLK
    listed_count = verticals.shape[1]
    position = lax.axis_index("ctx")
    logit_scale = 1.0 / math.sqrt(head_dim)
    owners = verticals // cache_blocks
    within = (verticals % cache_blocks)[:, :, None]
    flat_keys = cache_keys.reshape(kv_here, cache_blocks, BLK * head_dim)
    flat_values = cache_values.reshape(kv_here, cache_blocks, BLK * head_dim)
    picked = jnp.concatenate(
        [
            jnp.take_along_axis(flat_keys, within, axis=1),
            jnp.take_along_axis(flat_values, within, axis=1),
        ],
        axis=2,
    )
    holder = (owners == position)[:, :, None]
    offered = jnp.where(holder, picked.astype(jnp.float32), 0.0)
    columns = lax.psum(offered, "ctx").astype(jnp.bfloat16)
    column_keys = columns[:, :, : BLK * head_dim].reshape(kv_here, listed_count * BLK, head_dim)
    column_values = columns[:, :, BLK * head_dim :].reshape(kv_here, listed_count * BLK, head_dim)
    stretch_pair = jnp.concatenate([stretch_keys, stretch_values], axis=2)
    earlier = [passed_along(stretch_pair, "ctx", distance) for distance in range(SPAN, 0, -1)]
    extended = jnp.concatenate(earlier + [stretch_pair], axis=1)
    extended = extended.reshape(kv_here, (SPAN + 1) * query_blocks, BLK, 2 * head_dim)
    block_ids = jnp.arange(query_blocks, dtype=jnp.int32)
    inside = jnp.arange(BLK, dtype=jnp.int32)
    diagonal_ok = inside[None, :] <= inside[:, None]
    self_ok = jnp.broadcast_to(diagonal_ok[None], (query_blocks, BLK, BLK))
    offsets = slashes[0]
    source = SPAN * query_blocks + block_ids[:, None] - offsets[None, :]
    usable = position * query_blocks + block_ids[:, None] - offsets[None, :] >= 0
    band = extended[0][source].reshape(query_blocks, SPAN * BLK, 2 * head_dim)
    own_part = extended[0, SPAN * query_blocks :]
    nearby_pairs = jnp.concatenate([band, own_part], axis=1)
    band_ok = jnp.broadcast_to(
        jnp.repeat(usable, BLK, axis=1)[:, None, :], (query_blocks, BLK, SPAN * BLK)
    )
    allowed = jnp.concatenate([band_ok, self_ok], axis=2)
    outputs = attend_group(
        queries,
        column_keys[0],
        column_values[0],
        nearby_pairs[..., :head_dim],
        nearby_pairs[..., head_dim:],
        allowed,
        logit_scale,
    )
    return outputs


def solution(mesh):
    return jax.shard_map(
        local,
        mesh=mesh,
        in_specs=(
            P("head", "ctx", None),
            P("head", "ctx", None),
            P("head", "ctx", None),
            P("head", "ctx", None),
            P("head", "ctx", None),
            P("head", None),
            P("head", None),
        ),
        out_specs=P("head", "ctx", None),
        check_vma=False,
    )
```

profile of v0, /device:TPU:4, one launch (start us, length us, event | category | flops | bytes accessed | tf_op | source)
XLA Modules:
  0.0 373.9 jit_solution(3369027133924183563)
XLA Ops:
  0.0 1.7 constant_dynamic-update-slice_fusion.1
  1.7 1.7 constant_dynamic-update-slice_fusion
  3.4 6.9 %collective-permute-start = (bf16[1,1024,256]{2,1,0:T(8,128)(2,1)}, bf16[1,1024,256]{2,1,0:T(8,128)(2,1)}, u32[]{:S(2)}, u32[]{:S(2)}) collective-permute-start(bf16[1,1024,256]{2,1,0:T(8,128)(2,1)} %constant_dynamic-update-slice_fusion), channel_id=1, source_target_pairs={{0,32},{8,40},{16,48},{24,56},{32,64},{40,72},{48,80},{56,88},{64,... | collective-permute-start | bytes 1572872 | tf_op jit(solution)/shard_map/ppermute | solution.py:15
  10.3 4.2 %collective-permute-start.1 = (bf16[1,1024,256]{2,1,0:T(8,128)(2,1)}, bf16[1,1024,256]{2,1,0:T(8,128)(2,1)}, u32[]{:S(2)}, u32[]{:S(2)}) collective-permute-start(bf16[1,1024,256]{2,1,0:T(8,128)(2,1)} %constant_dynamic-update-slice_fusion), channel_id=1, source_target_pairs={{0,24},{8,32},{16,40},{24,48},{32,56},{40,64},{48,72},{56,80},{64,... | collective-permute-start | bytes 1572872 | tf_op jit(solution)/shard_map/ppermute | solution.py:15
  14.5 5.5 %collective-permute-start.2 = (bf16[1,1024,256]{2,1,0:T(8,128)(2,1)}, bf16[1,1024,256]{2,1,0:T(8,128)(2,1)}, u32[]{:S(2)}, u32[]{:S(2)}) collective-permute-start(bf16[1,1024,256]{2,1,0:T(8,128)(2,1)} %constant_dynamic-update-slice_fusion), channel_id=1, source_target_pairs={{0,16},{8,24},{16,32},{24,40},{32,48},{40,56},{48,64},{56,72},{64,... | collective-permute-start | bytes 1572872 | tf_op jit(solution)/shard_map/ppermute | solution.py:15
  20.0 3.5 collective-permute-start.3
  25.0 1.3 reshape.275
  26.3 1.3 reshape.280
  29.3 305.4 %all-reduce.1 = bf16[1,8,32768]{2,1,0:T(8,128)(2,1)S(1)} all-reduce(f32[1,8,32768]{2,1,0:T(8,128)S(1)} %convert_select_fusion), channel_id=1, replica_groups=mesh['ctx'=64,'head'=8] {'ctx'}, use_global_device_ids=true, to_apply=%region_0.2 | all-reduce | flops 262144 | bytes 1572864 | tf_op jit(solution)/shard_map/psum | solution.py:81
  334.9 0.8 squeeze_reshape.11
  336.2 1.1 constant_dynamic-update-slice_fusion.7
  337.3 1.1 constant_dynamic-update-slice_fusion.6
  338.4 1.1 constant_dynamic-update-slice_fusion.5
  339.5 1.1 constant_dynamic-update-slice_fusion.4
  340.7 0.8 slice_bitcast_fusion
  341.6 2.0 gather_fusion
  343.6 1.9 pad_maximum_fusion
  345.5 28.4 %while.10 = (s32[]{:T(128)}, bf16[4,1024,128]{2,1,0:T(8,128)(2,1)}, bf16[4,1024,128]{2,1,0:T(8,128)(2,1)}, bf16[1024,128]{1,0:T(8,128)(2,1)S(1)}, bf16[8,640,128...) while((s32[]{:T(128)}, bf16[4,1024,128]{2,1,0:T(8,128)(2,1)}, ...), condition=%wide.region_6.8_spmd, body=%wide.region_1.7_spmd.sunk | while | flops 885259264 | bytes 28258940 | solution.py:56
  345.5 1.0 constant_dynamic-slice_fusion.2
  348.0 0.8 fusion.34
  348.8 1.1 exponential_reduce_fusion.2
  349.9 1.2 fusion.35
  352.6 1.0 constant_dynamic-slice_fusion.2
  355.1 0.8 fusion.34
  355.9 1.1 exponential_reduce_fusion.2
  357.0 1.2 fusion.35
  359.7 1.0 constant_dynamic-slice_fusion.2
  363.0 1.1 exponential_reduce_fusion.2
  364.1 1.2 fusion.35
  366.8 1.0 constant_dynamic-slice_fusion.2
  370.1 1.1 exponential_reduce_fusion.2
  371.2 1.2 fusion.35
  (71 shorter events, 17.7 us)
Async XLA Ops:
  3.4 332.8 %collective-permute-start = (bf16[1,1024,256]{2,1,0:T(8,128)(2,1)}, bf16[1,1024,256]{2,1,0:T(8,128)(2,1)}, u32[]{:S(2)}, u32[]{:S(2)}) collective-permute-start(bf16[1,1024,256]{2,1,0:T(8,128)(2,1)} %constant_dynamic-update-slice_fusion), channel_id=1, source_target_pairs={{0,32},{8,40},{16,48},{24,56},{32,64},{40,72},{48,80},{56,88},{64,... | collective-permute-start | bytes 1572872 | tf_op jit(solution)/shard_map/ppermute | solution.py:15
  10.3 327.0 %collective-permute-start.1 = (bf16[1,1024,256]{2,1,0:T(8,128)(2,1)}, bf16[1,1024,256]{2,1,0:T(8,128)(2,1)}, u32[]{:S(2)}, u32[]{:S(2)}) collective-permute-start(bf16[1,1024,256]{2,1,0:T(8,128)(2,1)} %constant_dynamic-update-slice_fusion), channel_id=1, source_target_pairs={{0,24},{8,32},{16,40},{24,48},{32,56},{40,64},{48,72},{56,80},{64,... | collective-permute-start | bytes 1572872 | tf_op jit(solution)/shard_map/ppermute | solution.py:15
  14.5 323.9 %collective-permute-start.2 = (bf16[1,1024,256]{2,1,0:T(8,128)(2,1)}, bf16[1,1024,256]{2,1,0:T(8,128)(2,1)}, u32[]{:S(2)}, u32[]{:S(2)}) collective-permute-start(bf16[1,1024,256]{2,1,0:T(8,128)(2,1)} %constant_dynamic-update-slice_fusion), channel_id=1, source_target_pairs={{0,16},{8,24},{16,32},{24,40},{32,48},{40,56},{48,64},{56,72},{64,... | collective-permute-start | bytes 1572872 | tf_op jit(solution)/shard_map/ppermute | solution.py:15
  20.0 319.5 %collective-permute-start.3 = (bf16[1,1024,256]{2,1,0:T(8,128)(2,1)}, bf16[1,1024,256]{2,1,0:T(8,128)(2,1)}, u32[]{:S(2)}, u32[]{:S(2)}) collective-permute-start(bf16[1,1024,256]{2,1,0:T(8,128)(2,1)} %constant_dynamic-update-slice_fusion), channel_id=1, source_target_pairs={{0,8},{8,16},{16,24},{24,32},{32,40},{40,48},{48,56},{56,64},{64,7... | collective-permute-start | bytes 1572872 | tf_op jit(solution)/shard_map/ppermute | solution.py:15
  29.0 305.8 %copy-start.3 = (s32[1,4]{1,0:T(1,128)S(1)}, s32[1,4]{1,0:T(1,128)}, u32[]{:S(2)}) copy-start(s32[1,4]{1,0:T(1,128)} %param.17) | copy-start | bytes 52
  336.1 4.5 %copy-start = (bf16[1,1024,128]{2,1,0:T(8,128)(2,1)S(1)}, bf16[1,1024,128]{2,1,0:T(8,128)(2,1)}, u32[]{:S(2)}) copy-start(bf16[1,1024,128]{2,1,0:T(8,128)(2,1)} %param.14) | copy-start | bytes 786436
  336.2 4.5 %copy-start.1 = (bf16[1,1024,128]{2,1,0:T(8,128)(2,1)S(1)}, bf16[1,1024,128]{2,1,0:T(8,128)(2,1)}, u32[]{:S(2)}) copy-start(bf16[1,1024,128]{2,1,0:T(8,128)(2,1)} %param.15) | copy-start | bytes 786436
  348.8 1.1 copy-start.2
  355.9 1.1 copy-start.2
  363.0 1.1 copy-start.2
  370.1 1.1 copy-start.2
where the time goes:
time: 375 us; the launch traced here: 374 us
  blocking collectives  305 us (81%)
  local copies, waits for them, and re-layouts  22.8 us (6%)
  starting transfers between devices  20.1 us (5%)
  matrix products  13.8 us (4%)
  other arithmetic  11.3 us (3%)
    psum x1, blocking collectives, local(): columns = lax.psum(offered, 'ctx').astype(jnp.bfloat16)  305 us
    ppermute x4, starting transfers between devices, passed_along(): return lax.ppermute(x, axis, pairs)  20.1 us
  transfers between devices with their start and end apart: 4, of which 0 were waited for; matrix products, arithmetic and copies ran while one was open for 3% of the time, Pallas kernels for 0%

commit v1 on v0

v1 whole, which is shorter than its diff:
```python
import math

import jax
import jax.numpy as jnp
from jax import lax
from jax.experimental import pallas as pl
from jax.experimental.pallas import tpu as pltpu
from jax.sharding import PartitionSpec as P

BLK = 128
HD = 128
NV = 8
SPAN = 4
GROUP = 4
NY, NZ = 4, 8
LAST = 2 * NY * NZ
QROWS = 1024
QB = QROWS // BLK
CROWS = 2048
CB = CROWS // BLK
PART = BLK // NY
QUARTER = NV * PART
MESH = pl.DeviceIdType.MESH
COEF = math.log2(math.e) / math.sqrt(HD)
F32 = jnp.float32
BF16 = jnp.bfloat16


def tile(q, k, v, m, acc, keep=None):
    scores = lax.dot_general(q, k, (((1,), (1,)), ((), ())), preferred_element_type=F32)
    if keep is not None:
        scores = jnp.where(keep, scores, -jnp.inf)
    top = jnp.max(scores, axis=1, keepdims=True)
    new = top if m is None else jnp.maximum(m, top)
    p = jnp.exp2((scores - new) * COEF).astype(BF16)
    o = jnp.dot(p, v, preferred_element_type=F32)
    if m is not None:
        o = acc * jnp.exp2((m - new) * COEF) + o
    return new, o


def kernel(
    verts, slashes, q_hbm, ck_hbm, cv_hbm, sk_hbm, sv_hbm, out_hbm,
    q_v, cache, ring,
    gate, offer, pair, mixed, yb, zb1, zb2, far, far_v,
    near_k, near_v, acc_s, max_s, out_v,
    in_sem, out_sem, pair_sem, y_sem, z1_sem, z2_sem, ag_sem, fs_sem, a1_sem, a2_sem, s1_sem, s2_sem,
):
    me = lax.axis_index("ctx")
    c = lax.rem(me, 2)
    z = lax.rem(me // 2, NZ)
    y = me // (2 * NZ)

    def at(yy, zz, cc):
        return {"ctx": (yy * NZ + zz) * 2 + cc}

    sibling = at(y, z, 1 - c)
    y_peer = [at(lax.rem(y + k, NY), z, c) for k in range(1, NY)]
    z_peer = {k: at(y, lax.rem(z + k + NZ, NZ), c) for k in (-3, -1, 1, 3)}
    ahead = {"ctx": lax.rem(me + 2, LAST)}
    behind = {"ctx": lax.rem(me - 2 + LAST, LAST)}
    a2, s2, a1, s1, own = (ring.at[:, i * QB : (i + 1) * QB] for i in range(SPAN + 1))
    sends = me + 2 < LAST
    gets1 = me >= 2
    gets2 = me >= 4

    loads = [
        pltpu.make_async_copy(ck_hbm, cache.at[0], in_sem.at[0]),
        pltpu.make_async_copy(cv_hbm, cache.at[1], in_sem.at[1]),
        pltpu.make_async_copy(sk_hbm, own.at[0], in_sem.at[2]),
        pltpu.make_async_copy(sv_hbm, own.at[1], in_sem.at[3]),
        pltpu.make_async_copy(q_hbm, q_v, in_sem.at[4]),
    ]
    for load in loads:
        load.start()

    barrier = pltpu.get_barrier_semaphore()
    peers = [sibling] + y_peer + list(z_peer.values()) + [ahead, behind]
    for peer in peers:
        pl.semaphore_signal(barrier, inc=1, device_id=peer, device_id_type=MESH)

    loads[0].wait()
    loads[1].wait()
    for j in range(NV):
        block = lax.rem(verts[0, j], CB)
        mine = cache[pl.ds(c, 1), pl.ds(block, 1)].reshape(NY, PART, HD)
        other = cache[pl.ds(1 - c, 1), pl.ds(block, 1)].reshape(NY, PART, HD)
        pair[pl.ds(c, 1), :, j * PART : (j + 1) * PART, :] = mine[None]
        offer[:, j * PART : (j + 1) * PART, :] = other
    loads[2].wait()
    loads[3].wait()

    pl.semaphore_wait(barrier, len(peers))

    def remote(src, dst, send_sem, recv_sem, to):
        return pltpu.make_async_remote_copy(
            src_ref=src, dst_ref=dst, send_sem=send_sem, recv_sem=recv_sem, device_id=to, device_id_type=MESH
        )

    pair_out = remote(offer, pair.at[c], pair_sem.at[0], pair_sem.at[1], sibling)
    pair_in = remote(offer, pair.at[1 - c], pair_sem.at[0], pair_sem.at[1], sibling)
    pair_out.start()

    def hop(src, dst, sem, kv, to):
        return remote(src.at[kv], dst.at[kv], sem.at[kv], sem.at[2 + kv], to)

    @pl.when(sends)
    def _():
        for kv in (0, 1):
            hop(own, a1, a1_sem, kv, ahead).start()

    @pl.when(c == 0)
    def _():
        for kv in (0, 1):
            hop(own, s1, s1_sem, kv, sibling).start()

    @pl.when(jnp.logical_not(gets1))
    def _():
        ring[:, 2 * QB : 3 * QB] = jnp.zeros((2, QB, BLK, HD), BF16)

    @pl.when(jnp.logical_not(gets2))
    def _():
        ring[:, :QB] = jnp.zeros((2, QB, BLK, HD), BF16)

    gate[0] = jnp.zeros((BLK, HD), BF16)
    gate[1] = jnp.ones((BLK, HD), BF16)
    far_v[:, HD:] = jnp.ones((NY * QUARTER, HD), BF16)

    def owner(j):
        dev = lax.div(verts[0, j], CB)
        return lax.div(dev, 2 * NZ), lax.rem(lax.div(dev, 2), NZ), lax.rem(dev, 2)

    def one_if(lo, hi, x):
        return jnp.minimum(jnp.maximum(x - (lo - 1), 0), 1) * jnp.minimum(jnp.maximum(hi + 1 - x, 0), 1)

    def part(j):
        return slice(j * PART, (j + 1) * PART)

    pair_in.wait_recv()
    for j in range(NV):
        oc = owner(j)[2]
        mixed[:, part(j), :] = pair[pl.ds(oc, 1), :, part(j), :][0]
    y_out = []
    for k in range(1, NY):
        to = lax.rem(y + k, NY)
        y_out.append(remote(mixed.at[to], yb.at[y], y_sem.at[k - 1], y_sem.at[2 + k], y_peer[k - 1]))
        y_out[-1].start()
    yb[pl.ds(y, 1)] = mixed[pl.ds(y, 1)]
    for k in range(1, NY):
        frm = lax.rem(y + NY - k, NY)
        remote(mixed.at[frm], yb.at[frm], y_sem.at[k - 1], y_sem.at[2 + k], y_peer[k - 1]).wait_recv()

    for j in range(NV):
        oy = owner(j)[0]
        zb1[1, part(j), :] = yb[pl.ds(oy, 1), part(j), :][0]
    z1_out = [
        remote(zb1.at[1], zb1.at[0], z1_sem.at[0], z1_sem.at[2], z_peer[1]),
        remote(zb1.at[1], zb1.at[2], z1_sem.at[1], z1_sem.at[3], z_peer[-1]),
    ]
    for copy in z1_out:
        copy.start()
    for copy in z1_out:
        copy.wait_recv()
    for j in range(NV):
        off = lax.rem(owner(j)[1] - z + NZ, NZ)
        slot = 1 + one_if(1, 1, off) - one_if(NZ - 1, NZ - 1, off)
        zb2[1, part(j), :] = zb1[pl.ds(slot, 1), part(j), :][0]
    z2_out = [
        remote(zb2.at[1], zb2.at[0], z2_sem.at[0], z2_sem.at[2], z_peer[3]),
        remote(zb2.at[1], zb2.at[2], z2_sem.at[1], z2_sem.at[3], z_peer[-3]),
    ]
    for copy in z2_out:
        copy.start()

    for kv in (0, 1):

        @pl.when(gets1)
        def _():
            hop(own, a1, a1_sem, kv, behind).wait_recv()

        @pl.when(jnp.logical_and(gets1, sends))
        def _():
            hop(a1, a2, a2_sem, kv, ahead).start()

        @pl.when(c == 0)
        def _():
            hop(a1, s2, s2_sem, kv, sibling).start()

        @pl.when(c == 1)
        def _():
            hop(a1, s1, s1_sem, kv, sibling).start()

    for copy in z2_out:
        copy.wait_recv()
    for j in range(NV):
        off = lax.rem(owner(j)[1] - z + NZ, NZ)
        slot = 1 + one_if(2, 4, off) - one_if(5, 6, off)
        far[pl.ds(c, 1), pl.ds(y, 1), part(j), :] = zb2[pl.ds(slot, 1), part(j), :][None]

    ag_out = []
    for k in range(1, NY):
        ag_out.append(remote(far.at[c, y], far.at[c, y], ag_sem.at[k - 1], ag_sem.at[2 + k], y_peer[k - 1]))
        ag_out[-1].start()
    fs_out = [remote(far.at[c, y], far.at[c, y], fs_sem.at[0], fs_sem.at[NY], sibling)]
    fs_out[0].start()
    for k in range(1, NY):
        frm = lax.rem(y + NY - k, NY)
        remote(far.at[c, frm], far.at[c, frm], ag_sem.at[k - 1], ag_sem.at[2 + k], y_peer[k - 1]).wait_recv()
        fs_out.append(remote(far.at[c, frm], far.at[c, frm], fs_sem.at[k], fs_sem.at[NY + k], sibling))
        fs_out[-1].start()

    for kv in (0, 1):

        @pl.when(gets2)
        def _():
            hop(a1, a2, a2_sem, kv, behind).wait_recv()

        @pl.when(c == 1)
        def _():
            hop(a2, s2, s2_sem, kv, sibling).start()

    for kv in (0, 1):
        hop(own, s1, s1_sem, kv, sibling).wait_recv()
        hop(a1, s2, s2_sem, kv, sibling).wait_recv()

    loads[4].wait()

    def near_block(b, _):
        here = pl.multiple_of(b * BLK, BLK)
        last = SPAN * QB + b
        first = jnp.broadcast_to(ring[0, last, 0:16, :][0:1], (BLK, HD))
        for i in range(SPAN):
            s = slashes[0, i]
            counts = jnp.minimum(jnp.maximum(me * QB + b - s + 1, 0), 1)
            yes = gate[pl.ds(counts, 1)][0]
            no = gate[pl.ds(1 - counts, 1)][0]
            rows = slice(i * BLK, (i + 1) * BLK)
            near_k[b, rows, :] = ring[0, pl.ds(last - s, 1)][0] * yes + first * no
            near_v[b, rows, :HD] = ring[1, pl.ds(last - s, 1)][0] * yes
            near_v[b, rows, HD:] = yes
        rows = slice(SPAN * BLK, (SPAN + 1) * BLK)
        near_k[b, rows, :] = ring[0, last]
        near_v[b, rows, :HD] = ring[1, last]
        near_v[b, rows, HD:] = jnp.ones((BLK, HD), BF16)

        q = q_v[:, pl.ds(here, BLK), :].reshape(GROUP * BLK, HD)
        acc = m = None
        for lo, hi in ((0, 256), (256, 512), (512, 640)):
            keep = None
            if lo == SPAN * BLK:
                t = lax.rem(lax.broadcasted_iota(jnp.int32, (GROUP * BLK, BLK), 0), BLK)
                keep = lax.broadcasted_iota(jnp.int32, (GROUP * BLK, BLK), 1) <= t
            m, acc = tile(q, near_k[b, lo:hi, :], near_v[b, lo:hi, :], m, acc, keep)
        acc_s[:, pl.ds(here, BLK), :] = acc.reshape(GROUP, BLK, 2 * HD)
        max_s[:, pl.ds(here, BLK), :] = jnp.broadcast_to(m, (GROUP * BLK, HD)).reshape(GROUP, BLK, HD)
        return 0

    lax.fori_loop(0, QB, near_block, 0, unroll=True)

    fs_out[0].wait_recv()
    for k in range(1, NY):
        fs_out[k].wait_recv()
    far_v[:, :HD] = far[1].reshape(NY * QUARTER, HD)

    for t in range(NY):

        def far_head(h, _):
            m, acc = jnp.max(max_s[h], axis=1, keepdims=True), acc_s[h]
            m, acc = tile(q_v[h], far[0, t], far_v[t * QUARTER : (t + 1) * QUARTER, :], m, acc)
            if t < NY - 1:
                acc_s[h] = acc
                max_s[h] = jnp.broadcast_to(m, (QROWS, HD))
            else:
                out_v[h] = (acc[:, :HD] / acc[:, HD:]).astype(BF16)
                pltpu.make_async_copy(out_v.at[h], out_hbm.at[h], out_sem.at[h]).start()
            return 0

        lax.fori_loop(0, GROUP, far_head, 0, unroll=True)

    for h in range(GROUP):
        pltpu.make_async_copy(out_v.at[h], out_hbm.at[h], out_sem.at[h]).wait()
    for copy in [pair_out] + y_out + z1_out + z2_out + ag_out + fs_out:
        copy.wait_send()
    for kv in (0, 1):

        @pl.when(sends)
        def _():
            hop(own, a1, a1_sem, kv, ahead).wait_send()

        @pl.when(jnp.logical_and(gets1, sends))
        def _():
            hop(a1, a2, a2_sem, kv, ahead).wait_send()

        hop(own, s1, s1_sem, kv, sibling).wait_send()
        hop(a1, s2, s2_sem, kv, sibling).wait_send()


def local(queries, cache_keys, cache_values, stretch_keys, stretch_values, verticals, slashes):
    smem = pl.BlockSpec(memory_space=pltpu.SMEM)
    hbm = pl.BlockSpec(memory_space=pl.ANY)
    dma = pltpu.SemaphoreType.DMA
    vmem = pltpu.VMEM
    return pl.pallas_call(
        kernel,
        out_shape=jax.ShapeDtypeStruct((GROUP, QROWS, HD), BF16),
        in_specs=[smem, smem] + [hbm] * 5,
        out_specs=hbm,
        scratch_shapes=[
            vmem((GROUP, QROWS, HD), BF16),
            vmem((2, CB, BLK, HD), BF16),
            vmem((2, (SPAN + 1) * QB, BLK, HD), BF16),
            vmem((2, BLK, HD), BF16),
            vmem((NY, QUARTER, HD), BF16),
            vmem((2, NY, QUARTER, HD), BF16),
            vmem((NY, QUARTER, HD), BF16),
            vmem((NY, QUARTER, HD), BF16),
            vmem((3, QUARTER, HD), BF16),
            vmem((3, QUARTER, HD), BF16),
            vmem((2, NY, QUARTER, HD), BF16),
            vmem((NY * QUARTER, 2 * HD), BF16),
            vmem((QB, (SPAN + 1) * BLK, HD), BF16),
            vmem((QB, (SPAN + 1) * BLK, 2 * HD), BF16),
            vmem((GROUP, QROWS, 2 * HD), F32),
            vmem((GROUP, QROWS, HD), F32),
            vmem((GROUP, QROWS, HD), BF16),
            dma((5,)),
            dma((GROUP,)),
            dma((2,)),
            dma((6,)),
            dma((4,)),
            dma((4,)),
            dma((6,)),
            dma((2 * NY,)),
            dma((4,)),
            dma((4,)),
            dma((4,)),
            dma((4,)),
        ],
        compiler_params=pltpu.CompilerParams(collective_id=0, has_side_effects=True, vmem_limit_bytes=60 * 2**20),
        cost_estimate=pl.CostEstimate(flops=3500000000, bytes_accessed=4000000, transcendentals=7000000),
        name="sparse_attention",
    )(
        verticals,
        slashes,
        queries,
        cache_keys.reshape(CB, BLK, HD),
        cache_values.reshape(CB, BLK, HD),
        stretch_keys.reshape(QB, BLK, HD),
        stretch_values.reshape(QB, BLK, HD),
    )


def solution(mesh):
    return jax.shard_map(
        local,
        mesh=mesh,
        in_specs=(
            P("head", "ctx", None),
            P("head", "ctx", None),
            P("head", "ctx", None),
            P("head", "ctx", None),
            P("head", "ctx", None),
            P("head", None),
            P("head", None),
        ),
        out_specs=P("head", "ctx", None),
        check_vma=False,
    )
```

time: 375 us -> 72 us (0.19)
  the two profiles are of different devices: /device:TPU:4 before, /device:TPU:120 now
where the time goes in v1:
time: 72 us; the launch traced here: 71.8 us
  Pallas kernels  69.6 us (97%)
  local copies, waits for them, and re-layouts  2.26 us (3%)
    pallas_call x1, Pallas kernels, local(): pl.pallas_call(kernel, out_shape=jax.ShapeDtypeStruct((GROUP, QROWS, HD),...  69.6 us
    unnamed x1, local copies, waits for them, and re-layouts  2.26 us

profile of v1, /device:TPU:120, one launch (start us, length us, event | category | flops | bytes accessed | tf_op | source)
XLA Modules:
  0.0 71.8 jit_solution(5282780405855387589)
XLA Ops:
  0.0 69.6 %sparse_attention.1 = bf16[4,1024,128]{2,1,0:T(8,128)(2,1)} custom-call(s32[1,8]{1,0:T(1,128)} %verts.1, s32[1,4]{1,0:T(1,128)} %slashes.1, bf16[4,1024,128]{2,1,0:T(8,128)(2,1)} %q_hbm.1, bf16[16,128,128]{2,1,0:T(8,128)(2,1)} %bitcast.4, bf16[16,128,128]{2,1,0:T(8,128)(2,1)} %bitcast.5, bf16[8,128,128]{2,1,0:T(8,128)(2,1)} %bitcast.6, ...), custom_call_target="tpu_custom_call" | custom-call | flops 3500000000 | bytes 4000000 | tf_op jit(solution)/shard_map/sparse_attention/pallas_call | solution.py:303
  69.6 2.3 %copy.9 = bf16[4,1024,128]{2,1,0:T(8,128)(2,1)} copy(bf16[4,1024,128]{2,1,0:T(8,128)(2,1)} %sparse_attention.1) | data formatting | bytes 2097152

commit v2 on v1

v2 whole, which is shorter than its diff:
```python
import math

import jax
import jax.numpy as jnp
from jax import lax
from jax.experimental import pallas as pl
from jax.experimental.pallas import tpu as pltpu
from jax.sharding import PartitionSpec as P

BLK = 128
HD = 128
NV = 8
SPAN = 4
GROUP = 4
NY, NZ = 4, 8
LAST = 2 * NY * NZ
QROWS = 1024
QB = QROWS // BLK
CROWS = 2048
CB = CROWS // BLK
LASTBLOCK = LAST * CB - 1
PART = BLK // NY
FREE = 5
FIXED = NV - FREE
FROWS = FREE * PART
SROWS = FIXED * PART
MESH = pl.DeviceIdType.MESH
COEF = math.log2(math.e) / math.sqrt(HD)
F32 = jnp.float32
BF16 = jnp.bfloat16


def tile(q, k, v, m, acc, keep=None):
    scores = lax.dot_general(q, k, (((1,), (1,)), ((), ())), preferred_element_type=F32)
    if keep is not None:
        scores = jnp.where(keep, scores, -jnp.inf)
    top = jnp.max(scores, axis=1, keepdims=True)
    new = top if m is None else jnp.maximum(m, top)
    p = jnp.exp2((scores - new) * COEF).astype(BF16)
    o = jnp.dot(p, v, preferred_element_type=F32)
    if m is not None:
        o = acc * jnp.exp2((m - new) * COEF) + o
    return new, o


def one_if(lo, hi, x):
    return jnp.minimum(jnp.maximum(x - (lo - 1), 0), 1) * jnp.minimum(jnp.maximum(hi + 1 - x, 0), 1)


def sort_listed(verts):
    listed = [verts[0, j] for j in range(NV)]
    free = [one_if(CB, LASTBLOCK - 1, v) for v in listed]
    at = [0] * FREE
    count = 0
    for v, is_free in zip(listed, free):
        for t in range(FREE):
            at[t] = at[t] + v * is_free * one_if(t, t, count)
        count = count + is_free
    low = 0
    for v in listed:
        low = low + v * one_if(1, CB - 1, v)
    return at, low


def kernel(
    verts, slashes, q_hbm, ck_hbm, cv_hbm, sk_hbm, sv_hbm, out_hbm,
    q_v, cache, near, older, gate, offer, pair, mixed, yb, zb1, zb2, far, fixed,
    far_k, far_v, fix_k, fix_v, near_k, near_v, old_k, old_v, acc_s, max_s, out_v,
    in_sem, out_sem, pair_sem, y_sem, z1_sem, z2_sem, ag_sem, fs_sem,
    fy_sem, fz0_sem, fz7_sem, fg_sem, ff_sem, a1_sem, a2_sem, s1_sem, s2_sem,
):
    me = lax.axis_index("ctx")
    c = lax.rem(me, 2)
    z = lax.rem(lax.div(me, 2), NZ)
    y = lax.div(me, 2 * NZ)

    def at(yy, zz, cc):
        return {"ctx": (yy * NZ + zz) * 2 + cc}

    sibling = at(y, z, 1 - c)
    y_peer = [at(lax.rem(y + k, NY), z, c) for k in range(1, NY)]
    z_peer = [at(y, lax.rem(z + k, NZ), c) for k in range(NZ)]
    ahead = {"ctx": lax.rem(me + 2, LAST)}
    behind = {"ctx": lax.rem(me - 2 + LAST, LAST)}
    a1, s1, own = (near.at[:, i * QB : (i + 1) * QB] for i in range(3))
    a2, s2 = (older.at[:, i * QB : (i + 1) * QB] for i in range(2))
    sends = me + 2 < LAST
    gets1 = me >= 2
    gets2 = me >= 4
    first_z = z == 0
    last_z = z == NZ - 1

    loads = [
        pltpu.make_async_copy(ck_hbm, cache.at[0], in_sem.at[0]),
        pltpu.make_async_copy(cv_hbm, cache.at[1], in_sem.at[1]),
        pltpu.make_async_copy(sk_hbm, own.at[0], in_sem.at[2]),
        pltpu.make_async_copy(sv_hbm, own.at[1], in_sem.at[3]),
        pltpu.make_async_copy(q_hbm, q_v, in_sem.at[4]),
    ]
    for load in loads:
        load.start()

    barrier = pltpu.get_barrier_semaphore()
    peers = [sibling] + y_peer + z_peer[1:] + [ahead, behind]
    for peer in peers:
        pl.semaphore_signal(barrier, inc=1, device_id=peer, device_id_type=MESH)

    free, low = sort_listed(verts)
    offered = [lax.rem(v, CB) for v in free] + [0, low, CB - 1]

    def part(j):
        return slice(j * PART, (j + 1) * PART)

    loads[0].wait()
    loads[1].wait()
    for j, block in enumerate(offered):
        pair[pl.ds(c, 1), :, part(j), :] = cache[pl.ds(c, 1), pl.ds(block, 1)].reshape(1, NY, PART, HD)
        offer[:, part(j), :] = cache[pl.ds(1 - c, 1), pl.ds(block, 1)].reshape(NY, PART, HD)
    pl.semaphore_wait(barrier, len(peers))

    def remote(src, dst, send_sem, recv_sem, to):
        return pltpu.make_async_remote_copy(
            src_ref=src, dst_ref=dst, send_sem=send_sem, recv_sem=recv_sem, device_id=to, device_id_type=MESH
        )

    pair_out = remote(offer, pair.at[c], pair_sem.at[0], pair_sem.at[1], sibling)
    pair_out.start()
    loads[2].wait()
    loads[3].wait()

    def hop(src, dst, sem, kv, to):
        return remote(src.at[kv], dst.at[kv], sem.at[kv], sem.at[2 + kv], to)

    @pl.when(sends)
    def _():
        for kv in (0, 1):
            hop(own, a1, a1_sem, kv, ahead).start()

    @pl.when(jnp.logical_not(gets1))
    def _():
        near[:, :QB] = jnp.zeros((2, QB, BLK, HD), BF16)

    @pl.when(jnp.logical_not(gets2))
    def _():
        older[:, :QB] = jnp.zeros((2, QB, BLK, HD), BF16)

    gate[0] = jnp.zeros((BLK, HD), BF16)
    gate[1] = jnp.ones((BLK, HD), BF16)
    far_v[:, HD:] = jnp.ones((NY * FROWS, HD), BF16)
    fix_v[:, HD:] = jnp.ones((NY * SROWS, HD), BF16)

    owner = [lax.div(v, CB) for v in free]
    owner_y = [lax.div(d, 2 * NZ) for d in owner]
    owner_z = [lax.rem(lax.div(d, 2), NZ) for d in owner]
    owner_c = [lax.rem(d, 2) for d in owner]

    remote(offer, pair.at[1 - c], pair_sem.at[0], pair_sem.at[1], sibling).wait_recv()
    for j in range(FREE):
        mixed[:, part(j), :] = pair[pl.ds(owner_c[j], 1), :, part(j), :][0]
    y_out = []
    for k in range(1, NY):
        to = lax.rem(y + k, NY)
        y_out.append(
            remote(mixed.at[to, :FROWS], yb.at[y], y_sem.at[k - 1], y_sem.at[2 + k], y_peer[k - 1])
        )
        y_out[-1].start()
    yb[pl.ds(y, 1)] = mixed[pl.ds(y, 1), :FROWS, :]
    mixed[:, FROWS : FROWS + 2 * PART, :] = pair[0, :, FROWS : FROWS + 2 * PART, :]
    mixed[:, FROWS + 2 * PART :, :] = pair[1, :, FROWS + 2 * PART :, :]

    @pl.when(c == 0)
    def _():
        for kv in (0, 1):
            hop(own, s1, s1_sem, kv, sibling).start()

    halves = (
        (jnp.logical_and(first_z, y == 0), first_z, 0, 2 * PART, fz0_sem),
        (jnp.logical_and(last_z, y == NY - 1), last_z, 2 * PART, SROWS, fz7_sem),
    )

    def fixed_y(k, lo, hi):
        to = lax.rem(y + k, NY)
        return remote(
            mixed.at[to, FROWS + lo : FROWS + hi], fixed.at[c, to, lo:hi], fy_sem.at[k - 1], fy_sem.at[3], y_peer[k - 1]
        )

    def fixed_z(k, lo, hi, sem):
        return remote(fixed.at[c, y, lo:hi], fixed.at[c, y, lo:hi], sem.at[k], sem.at[0], z_peer[k])

    for root, line, lo, hi, sem in halves:

        @pl.when(root)
        def _():
            for k in range(1, NY):
                fixed_y(k, lo, hi).start()
            fixed[pl.ds(c, 1), pl.ds(y, 1), lo:hi, :] = mixed[pl.ds(y, 1), FROWS + lo : FROWS + hi, :][None]

    for k in range(1, NY):
        frm = lax.rem(y + NY - k, NY)
        remote(mixed.at[frm, :FROWS], yb.at[frm], y_sem.at[k - 1], y_sem.at[2 + k], y_peer[k - 1]).wait_recv()
    for j in range(FREE):
        zb1[1, part(j), :] = yb[pl.ds(owner_y[j], 1), part(j), :][0]
    z1_out = [
        remote(zb1.at[1], zb1.at[0], z1_sem.at[0], z1_sem.at[2], z_peer[1]),
        remote(zb1.at[1], zb1.at[2], z1_sem.at[1], z1_sem.at[3], z_peer[NZ - 1]),
    ]
    for copy in z1_out:
        copy.start()

    for root, line, lo, hi, sem in halves:

        @pl.when(jnp.logical_and(line, jnp.logical_not(root)))
        def _():
            fixed_y(1, lo, hi).wait_recv()

        @pl.when(line)
        def _():
            for k in range(1, NZ):
                fixed_z(k, lo, hi, sem).start()

    for copy in z1_out:
        copy.wait_recv()
    off = [lax.rem(o - z + NZ, NZ) for o in owner_z]
    for j in range(FREE):
        slot = 1 + one_if(1, 1, off[j]) - one_if(NZ - 1, NZ - 1, off[j])
        zb2[1, part(j), :] = zb1[pl.ds(slot, 1), part(j), :][0]
    z2_out = [
        remote(zb2.at[1], zb2.at[0], z2_sem.at[0], z2_sem.at[2], z_peer[3]),
        remote(zb2.at[1], zb2.at[2], z2_sem.at[1], z2_sem.at[3], z_peer[NZ - 3]),
    ]
    for copy in z2_out:
        copy.start()

    for root, line, lo, hi, sem in halves:

        @pl.when(jnp.logical_not(line))
        def _():
            fixed_z(1, lo, hi, sem).wait_recv()

    def gather(buf, sem, k):
        return remote(buf.at[c, y], buf.at[c, y], sem.at[k - 1], sem.at[2 + k], y_peer[k - 1])

    def gathered(buf, sem, k):
        frm = lax.rem(y + NY - k, NY)
        return remote(buf.at[c, frm], buf.at[c, frm], sem.at[k - 1], sem.at[2 + k], y_peer[k - 1])

    def share(buf, sem, k):
        frm = lax.rem(y + NY - k, NY)
        return remote(buf.at[c, frm], buf.at[c, frm], sem.at[k], sem.at[NY + k], sibling)

    def shared(buf, sem, k):
        frm = lax.rem(y + NY - k, NY)
        return remote(buf.at[1 - c, frm], buf.at[1 - c, frm], sem.at[k], sem.at[NY + k], sibling)

    for k in range(1, NY):
        gather(fixed, fg_sem, k).start()
    share(fixed, ff_sem, 0).start()

    for kv in (0, 1):

        @pl.when(gets1)
        def _():
            hop(own, a1, a1_sem, kv, behind).wait_recv()

        @pl.when(c == 0)
        def _():
            hop(a1, s2, s2_sem, kv, sibling).start()

        @pl.when(c == 1)
        def _():
            hop(a1, s1, s1_sem, kv, sibling).start()

    for k in range(1, NY):
        gathered(fixed, fg_sem, k).wait_recv()
        share(fixed, ff_sem, k).start()

    for copy in z2_out:
        copy.wait_recv()
    for j in range(FREE):
        slot = 1 + one_if(2, 4, off[j]) - one_if(5, 6, off[j])
        far[pl.ds(c, 1), pl.ds(y, 1), part(j), :] = zb2[pl.ds(slot, 1), part(j), :][None]
    for k in range(1, NY):
        gather(far, ag_sem, k).start()
    share(far, fs_sem, 0).start()

    @pl.when(jnp.logical_and(gets1, sends))
    def _():
        for kv in (0, 1):
            hop(a1, a2, a2_sem, kv, ahead).start()

    loads[4].wait()
    for kv in (0, 1):
        hop(own, s1, s1_sem, kv, sibling).wait_recv()
    for k in range(NY):
        shared(fixed, ff_sem, k).wait_recv()
    fix_k[...] = fixed[0].reshape(NY * SROWS, HD)
    fix_v[:, :HD] = fixed[1].reshape(NY * SROWS, HD)
    older[:, 2 * QB :] = near[:, :QB]

    def diagonal(b, i, ring, offset, k_ref, v_ref, rows):
        s = slashes[0, i]
        counts = jnp.minimum(jnp.maximum(me * QB + b - s + 1, 0), 1)
        yes = gate[pl.ds(counts, 1)][0]
        no = gate[pl.ds(1 - counts, 1)][0]
        head_row = jnp.broadcast_to(near[0, 2 * QB + b, 0:16, :][0:1], (BLK, HD))
        block = pl.ds(jnp.minimum(jnp.maximum(offset + b - s, 0), 3 * QB - 1), 1)
        k_ref[b, rows, :] = ring[0, block][0] * yes + head_row * no
        v_ref[b, rows, :HD] = ring[1, block][0] * yes
        v_ref[b, rows, HD:] = yes

    def block_rows(b):
        return pl.ds(pl.multiple_of(b * BLK, BLK), BLK)

    def near_block(b, _):
        diagonal(b, 0, near, 2 * QB, near_k, near_v, slice(0, BLK))
        diagonal(b, 1, near, 2 * QB, near_k, near_v, slice(BLK, 2 * BLK))
        near_k[b, 2 * BLK : 3 * BLK, :] = near[0, 2 * QB + b]
        near_v[b, 2 * BLK : 3 * BLK, :HD] = near[1, 2 * QB + b]
        near_v[b, 2 * BLK : 3 * BLK, HD:] = jnp.ones((BLK, HD), BF16)
        near_k[b, 3 * BLK :, :] = fix_k[:BLK, :]
        near_v[b, 3 * BLK :, :] = fix_v[:BLK, :]
        q = q_v[:, block_rows(b), :].reshape(GROUP * BLK, HD)
        t = lax.rem(lax.broadcasted_iota(jnp.int32, (GROUP * BLK, 2 * BLK), 0), BLK)
        u = lax.broadcasted_iota(jnp.int32, (GROUP * BLK, 2 * BLK), 1)
        keep = jnp.logical_or(u <= t, u >= BLK)
        m, acc = tile(q, near_k[b, 2 * BLK :, :], near_v[b, 2 * BLK :, :], None, None, keep)
        m, acc = tile(q, near_k[b, : 2 * BLK, :], near_v[b, : 2 * BLK, :], m, acc)
        m, acc = tile(q, fix_k[BLK:, :], fix_v[BLK:, :], m, acc)
        acc_s[:, block_rows(b), :] = acc.reshape(GROUP, BLK, 2 * HD)
        max_s[:, block_rows(b), :] = jnp.broadcast_to(m, (GROUP * BLK, HD)).reshape(GROUP, BLK, HD)
        return 0

    lax.fori_loop(0, QB, near_block, 0, unroll=True)

    for k in range(1, NY):
        gathered(far, ag_sem, k).wait_recv()
        share(far, fs_sem, k).start()
    for k in range(NY):
        shared(far, fs_sem, k).wait_recv()
    far_k[...] = far[0].reshape(NY * FROWS, HD)
    far_v[:, :HD] = far[1].reshape(NY * FROWS, HD)

    def far_head(h, _):
        q = q_v[h]
        m, acc = jnp.max(max_s[h], axis=1, keepdims=True), acc_s[h]
        for lo in range(0, NY * FROWS, 2 * BLK):
            hi = min(lo + 2 * BLK, NY * FROWS)
            m, acc = tile(q, far_k[lo:hi, :], far_v[lo:hi, :], m, acc)
        acc_s[h] = acc
        max_s[h] = jnp.broadcast_to(m, (QROWS, HD))
        return 0

    lax.fori_loop(0, GROUP, far_head, 0, unroll=True)

    for kv in (0, 1):

        @pl.when(gets2)
        def _():
            hop(a1, a2, a2_sem, kv, behind).wait_recv()

        @pl.when(c == 1)
        def _():
            hop(a2, s2, s2_sem, kv, sibling).start()

    for kv in (0, 1):
        hop(a1, s2, s2_sem, kv, sibling).wait_recv()

    def old_block(b, _):
        diagonal(b, 2, older, SPAN * QB, old_k, old_v, slice(0, BLK))
        diagonal(b, 3, older, SPAN * QB, old_k, old_v, slice(BLK, 2 * BLK))
        rows = block_rows(b)
        q = q_v[:, rows, :].reshape(GROUP * BLK, HD)
        m = jnp.max(max_s[:, rows, :].reshape(GROUP * BLK, HD), axis=1, keepdims=True)
        m, acc = tile(q, old_k[b], old_v[b], m, acc_s[:, rows, :].reshape(GROUP * BLK, 2 * HD))
        out_v[:, rows, :] = (acc[:, :HD] / acc[:, HD:]).astype(BF16).reshape(GROUP, BLK, HD)
        pltpu.make_async_copy(out_v.at[:, rows], out_hbm.at[:, rows], out_sem.at[b]).start()
        return 0

    lax.fori_loop(0, QB, old_block, 0, unroll=True)

    for b in range(QB):
        rows = pl.ds(b * BLK, BLK)
        pltpu.make_async_copy(out_v.at[:, rows], out_hbm.at[:, rows], out_sem.at[b]).wait()
    for copy in [pair_out] + y_out + z1_out + z2_out:
        copy.wait_send()
    for k in range(1, NY):
        gather(fixed, fg_sem, k).wait_send()
        gather(far, ag_sem, k).wait_send()
    for k in range(NY):
        share(fixed, ff_sem, k).wait_send()
        share(far, fs_sem, k).wait_send()
    for root, line, lo, hi, sem in halves:

        @pl.when(root)
        def _():
            for k in range(1, NY):
                fixed_y(k, lo, hi).wait_send()

        @pl.when(line)
        def _():
            for k in range(1, NZ):
                fixed_z(k, lo, hi, sem).wait_send()

    for kv in (0, 1):

        @pl.when(sends)
        def _():
            hop(own, a1, a1_sem, kv, ahead).wait_send()

        @pl.when(jnp.logical_and(gets1, sends))
        def _():
            hop(a1, a2, a2_sem, kv, ahead).wait_send()

        hop(own, s1, s1_sem, kv, sibling).wait_send()
        hop(a1, s2, s2_sem, kv, sibling).wait_send()


def local(queries, cache_keys, cache_values, stretch_keys, stretch_values, verticals, slashes):
    smem = pl.BlockSpec(memory_space=pltpu.SMEM)
    hbm = pl.BlockSpec(memory_space=pl.ANY)
    dma = pltpu.SemaphoreType.DMA
    vmem = pltpu.VMEM
    return pl.pallas_call(
        kernel,
        out_shape=jax.ShapeDtypeStruct((GROUP, QROWS, HD), BF16),
        in_specs=[smem, smem] + [hbm] * 5,
        out_specs=hbm,
        scratch_shapes=[
            vmem((GROUP, QROWS, HD), BF16),
            vmem((2, CB, BLK, HD), BF16),
            vmem((2, 3 * QB, BLK, HD), BF16),
            vmem((2, 3 * QB, BLK, HD), BF16),
            vmem((2, BLK, HD), BF16),
            vmem((NY, NV * PART, HD), BF16),
            vmem((2, NY, NV * PART, HD), BF16),
            vmem((NY, NV * PART, HD), BF16),
            vmem((NY, FROWS, HD), BF16),
            vmem((3, FROWS, HD), BF16),
            vmem((3, FROWS, HD), BF16),
            vmem((2, NY, FROWS, HD), BF16),
            vmem((2, NY, SROWS, HD), BF16),
            vmem((NY * FROWS, HD), BF16),
            vmem((NY * FROWS, 2 * HD), BF16),
            vmem((NY * SROWS, HD), BF16),
            vmem((NY * SROWS, 2 * HD), BF16),
            vmem((QB, 4 * BLK, HD), BF16),
            vmem((QB, 4 * BLK, 2 * HD), BF16),
            vmem((QB, 2 * BLK, HD), BF16),
            vmem((QB, 2 * BLK, 2 * HD), BF16),
            vmem((GROUP, QROWS, 2 * HD), F32),
            vmem((GROUP, QROWS, HD), F32),
            vmem((GROUP, QROWS, HD), BF16),
            dma((5,)),
            dma((QB,)),
            dma((2,)),
            dma((6,)),
            dma((4,)),
            dma((4,)),
            dma((6,)),
            dma((2 * NY,)),
            dma((4,)),
            dma((NZ,)),
            dma((NZ,)),
            dma((6,)),
            dma((2 * NY,)),
            dma((4,)),
            dma((4,)),
            dma((4,)),
            dma((4,)),
        ],
        compiler_params=pltpu.CompilerParams(collective_id=0, has_side_effects=True, vmem_limit_bytes=60 * 2**20),
        cost_estimate=pl.CostEstimate(flops=3500000000, bytes_accessed=4000000, transcendentals=7000000),
        name="sparse_attention",
    )(
        verticals,
        slashes,
        queries,
        cache_keys.reshape(CB, BLK, HD),
        cache_values.reshape(CB, BLK, HD),
        stretch_keys.reshape(QB, BLK, HD),
        stretch_values.reshape(QB, BLK, HD),
    )


def solution(mesh):
    return jax.shard_map(
        local,
        mesh=mesh,
        in_specs=(
            P("head", "ctx", None),
            P("head", "ctx", None),
            P("head", "ctx", None),
            P("head", "ctx", None),
            P("head", "ctx", None),
            P("head", None),
            P("head", None),
        ),
        out_specs=P("head", "ctx", None),
        check_vma=False,
    )
```

time: 72 us -> 55.2 us (0.77)
  the two profiles are of different devices: /device:TPU:120 before, /device:TPU:4 now
where the time goes in v2:
time: 55.2 us; the launch traced here: 55 us
  Pallas kernels  52.7 us (95%)
  local copies, waits for them, and re-layouts  2.26 us (4%)
    pallas_call x1, Pallas kernels, local(): pl.pallas_call(kernel, out_shape=jax.ShapeDtypeStruct((GROUP, QROWS, HD),...  52.7 us
    unnamed x1, local copies, waits for them, and re-layouts  2.26 us

profile of v2, /device:TPU:4, one launch (start us, length us, event | category | flops | bytes accessed | tf_op | source)
XLA Modules:
  0.0 55.0 jit_solution(11502494333440453648)
XLA Ops:
  0.0 52.7 %sparse_attention.1 = bf16[4,1024,128]{2,1,0:T(8,128)(2,1)} custom-call(s32[1,8]{1,0:T(1,128)} %verts.1, s32[1,4]{1,0:T(1,128)} %slashes.1, bf16[4,1024,128]{2,1,0:T(8,128)(2,1)} %q_hbm.1, bf16[16,128,128]{2,1,0:T(8,128)(2,1)} %bitcast.4, bf16[16,128,128]{2,1,0:T(8,128)(2,1)} %bitcast.5, bf16[8,128,128]{2,1,0:T(8,128)(2,1)} %bitcast.6, ...), custom_call_target="tpu_custom_call" | custom-call | flops 3500000000 | bytes 4000000 | tf_op jit(solution)/shard_map/sparse_attention/pallas_call | solution.py:423
  52.7 2.3 %copy.9 = bf16[4,1024,128]{2,1,0:T(8,128)(2,1)} copy(bf16[4,1024,128]{2,1,0:T(8,128)(2,1)} %sparse_attention.1) | data formatting | bytes 2097152

commit v3 on v2

--- a/solution.py
+++ b/solution.py
@@ -64,10 +64,10 @@
 
 def kernel(
     verts, slashes, q_hbm, ck_hbm, cv_hbm, sk_hbm, sv_hbm, out_hbm,
-    q_v, cache, near, older, gate, offer, pair, mixed, yb, zb1, zb2, far, fixed,
+    q_v, cache, near, older, stop, gate, offer, pair, mixed, yb, zb1, zb2, far, fixed,
     far_k, far_v, fix_k, fix_v, near_k, near_v, old_k, old_v, acc_s, max_s, out_v,
     in_sem, out_sem, pair_sem, y_sem, z1_sem, z2_sem, ag_sem, fs_sem,
-    fy_sem, fz0_sem, fz7_sem, fg_sem, ff_sem, a1_sem, a2_sem, s1_sem, s2_sem,
+    fy_sem, fz0_sem, fz7_sem, fg_sem, ff_sem, a1_sem, a2_sem, s1_sem, s2_sem, stop_sem,
 ):
     me = lax.axis_index("ctx")
     c = lax.rem(me, 2)
@@ -131,10 +131,70 @@
     def hop(src, dst, sem, kv, to):
         return remote(src.at[kv], dst.at[kv], sem.at[kv], sem.at[2 + kv], to)
 
-    @pl.when(sends)
-    def _():
+    in_row = z < NZ - 1
+    leaves_row = jnp.logical_and(last_z, sends)
+    passes_keys = jnp.logical_and(first_z, y < NY - 1)
+    passes_values = jnp.logical_and(last_z, y > 0)
+    corner = (z_peer[1], y_peer[0])
+
+    def leg1(i, kv):
+        return remote((own, a1)[i].at[kv], stop.at[i], (a1_sem, a2_sem)[i].at[kv], stop_sem.at[i], corner[kv])
+
+    def leg2(i, kv):
+        sem = (a1_sem, a2_sem)[i].at[2 + kv]
+        return remote(stop.at[i], (a1, a2)[i].at[kv], stop_sem.at[2 + i], sem, corner[1 - kv])
+
+    def stretch_step(step):
         for kv in (0, 1):
-            hop(own, a1, a1_sem, kv, ahead).start()
+            if step == 0:
+
+                @pl.when(jnp.logical_and(sends, in_row))
+                def _():
+                    hop(own, a1, a1_sem, kv, ahead).start()
+
+            if step == 0:
+
+                @pl.when(leaves_row)
+                def _():
+                    leg1(0, kv).start()
+
+            if step == (1, 2)[kv]:
+
+                @pl.when((passes_keys, passes_values)[kv])
+                def _():
+                    leg1(0, kv).wait_recv()
+                    leg2(0, kv).start()
+
+            if step == 4:
+
+                @pl.when(gets1)
+                def _():
+                    hop(own, a1, a1_sem, kv, behind).wait_recv()
+
+                @pl.when(c == 0)
+                def _():
+                    hop(a1, s2, s2_sem, kv, sibling).start()
+
+                @pl.when(c == 1)
+                def _():
+                    hop(a1, s1, s1_sem, kv, sibling).start()
+
+                @pl.when(jnp.logical_and(gets1, in_row))
+                def _():
+                    hop(a1, a2, a2_sem, kv, ahead).start()
+
+                @pl.when(leaves_row)
+                def _():
+                    leg1(1, kv).start()
+
+            if step == 5:
+
+                @pl.when((passes_keys, passes_values)[kv])
+                def _():
+                    leg1(1, kv).wait_recv()
+                    leg2(1, kv).start()
+
+    stretch_step(0)
 
     @pl.when(jnp.logical_not(gets1))
     def _():
@@ -198,6 +258,7 @@
     for k in range(1, NY):
         frm = lax.rem(y + NY - k, NY)
         remote(mixed.at[frm, :FROWS], yb.at[frm], y_sem.at[k - 1], y_sem.at[2 + k], y_peer[k - 1]).wait_recv()
+    stretch_step(1)
     for j in range(FREE):
         zb1[1, part(j), :] = yb[pl.ds(owner_y[j], 1), part(j), :][0]
     z1_out = [
@@ -220,6 +281,7 @@
 
     for copy in z1_out:
         copy.wait_recv()
+    stretch_step(2)
     off = [lax.rem(o - z + NZ, NZ) for o in owner_z]
     for j in range(FREE):
         slot = 1 + one_if(1, 1, off[j]) - one_if(NZ - 1, NZ - 1, off[j])
@@ -256,20 +318,6 @@
         gather(fixed, fg_sem, k).start()
     share(fixed, ff_sem, 0).start()
 
-    for kv in (0, 1):
-
-        @pl.when(gets1)
-        def _():
-            hop(own, a1, a1_sem, kv, behind).wait_recv()
-
-        @pl.when(c == 0)
-        def _():
-            hop(a1, s2, s2_sem, kv, sibling).start()
-
-        @pl.when(c == 1)
-        def _():
-            hop(a1, s1, s1_sem, kv, sibling).start()
-
     for k in range(1, NY):
         gathered(fixed, fg_sem, k).wait_recv()
         share(fixed, ff_sem, k).start()
@@ -283,10 +331,7 @@
         gather(far, ag_sem, k).start()
     share(far, fs_sem, 0).start()
 
-    @pl.when(jnp.logical_and(gets1, sends))
-    def _():
-        for kv in (0, 1):
-            hop(a1, a2, a2_sem, kv, ahead).start()
+    stretch_step(4)
 
     loads[4].wait()
     for kv in (0, 1):
@@ -335,6 +380,7 @@
     for k in range(1, NY):
         gathered(far, ag_sem, k).wait_recv()
         share(far, fs_sem, k).start()
+    stretch_step(5)
     for k in range(NY):
         shared(far, fs_sem, k).wait_recv()
     far_k[...] = far[0].reshape(NY * FROWS, HD)
@@ -410,6 +456,11 @@
         @pl.when(jnp.logical_and(gets1, sends))
         def _():
             hop(a1, a2, a2_sem, kv, ahead).wait_send()
+
+        @pl.when((passes_keys, passes_values)[kv])
+        def _():
+            for i in (0, 1):
+                leg2(i, kv).wait_send()
 
         hop(own, s1, s1_sem, kv, sibling).wait_send()
         hop(a1, s2, s2_sem, kv, sibling).wait_send()
@@ -430,6 +481,7 @@
             vmem((2, CB, BLK, HD), BF16),
             vmem((2, 3 * QB, BLK, HD), BF16),
             vmem((2, 3 * QB, BLK, HD), BF16),
+            vmem((2, QB, BLK, HD), BF16),
             vmem((2, BLK, HD), BF16),
             vmem((NY, NV * PART, HD), BF16),
             vmem((2, NY, NV * PART, HD), BF16),
@@ -467,6 +519,7 @@
             dma((4,)),
             dma((4,)),
             dma((4,)),
+            dma((4,)),
         ],
         compiler_params=pltpu.CompilerParams(collective_id=0, has_side_effects=True, vmem_limit_bytes=60 * 2**20),
         cost_estimate=pl.CostEstimate(flops=3500000000, bytes_accessed=4000000, transcendentals=7000000),

time: 55.2 us -> 53.2 us (0.964)
  the two profiles are of different devices: /device:TPU:4 before, /device:TPU:54 now
where the time goes in v3:
time: 53.2 us; the launch traced here: 53 us
  Pallas kernels  50.8 us (95%)
  local copies, waits for them, and re-layouts  2.26 us (4%)
    pallas_call x1, Pallas kernels, local(): pl.pallas_call(kernel, out_shape=jax.ShapeDtypeStruct((GROUP, QROWS, HD),...  50.8 us
    unnamed x1, local copies, waits for them, and re-layouts  2.26 us

profile of v3, /device:TPU:54, one launch (start us, length us, event | category | flops | bytes accessed | tf_op | source)
XLA Modules:
  0.0 53.0 jit_solution(11758924874908096139)
XLA Ops:
  0.0 50.8 %sparse_attention.1 = bf16[4,1024,128]{2,1,0:T(8,128)(2,1)} custom-call(s32[1,8]{1,0:T(1,128)} %verts.1, s32[1,4]{1,0:T(1,128)} %slashes.1, bf16[4,1024,128]{2,1,0:T(8,128)(2,1)} %q_hbm.1, bf16[16,128,128]{2,1,0:T(8,128)(2,1)} %bitcast.4, bf16[16,128,128]{2,1,0:T(8,128)(2,1)} %bitcast.5, bf16[8,128,128]{2,1,0:T(8,128)(2,1)} %bitcast.6, ...), custom_call_target="tpu_custom_call" | custom-call | flops 3500000000 | bytes 4000000 | tf_op jit(solution)/shard_map/sparse_attention/pallas_call | solution.py:474
  50.8 2.3 %copy.9 = bf16[4,1024,128]{2,1,0:T(8,128)(2,1)} copy(bf16[4,1024,128]{2,1,0:T(8,128)(2,1)} %sparse_attention.1) | data formatting | bytes 2097152

commit v4 on v3

--- a/solution.py
+++ b/solution.py
@@ -383,6 +383,19 @@
     stretch_step(5)
     for k in range(NY):
         shared(far, fs_sem, k).wait_recv()
+
+    def receive_relayed(where):
+        for kv in (0, 1):
+
+            @pl.when(jnp.logical_and(gets2, where))
+            def _():
+                hop(a1, a2, a2_sem, kv, behind).wait_recv()
+
+            @pl.when(jnp.logical_and(c == 1, where))
+            def _():
+                hop(a2, s2, s2_sem, kv, sibling).start()
+
+    receive_relayed(z > 0)
     far_k[...] = far[0].reshape(NY * FROWS, HD)
     far_v[:, :HD] = far[1].reshape(NY * FROWS, HD)
 
@@ -398,16 +411,7 @@
 
     lax.fori_loop(0, GROUP, far_head, 0, unroll=True)
 
-    for kv in (0, 1):
-
-        @pl.when(gets2)
-        def _():
-            hop(a1, a2, a2_sem, kv, behind).wait_recv()
-
-        @pl.when(c == 1)
-        def _():
-            hop(a2, s2, s2_sem, kv, sibling).start()
-
+    receive_relayed(first_z)
     for kv in (0, 1):
         hop(a1, s2, s2_sem, kv, sibling).wait_recv()
 
@@ -475,7 +479,7 @@
         kernel,
         out_shape=jax.ShapeDtypeStruct((GROUP, QROWS, HD), BF16),
         in_specs=[smem, smem] + [hbm] * 5,
-        out_specs=hbm,
+        out_specs=pl.BlockSpec(memory_space=pltpu.HBM),
         scratch_shapes=[
             vmem((GROUP, QROWS, HD), BF16),
             vmem((2, CB, BLK, HD), BF16),

time: 53.2 us -> 54 us (1.015)
  the two profiles are of different devices: /device:TPU:54 before, /device:TPU:252 now
where the time goes in v4:
time: 54 us; the launch traced here: 53.8 us
  Pallas kernels  51.5 us (95%)
  local copies, waits for them, and re-layouts  2.26 us (4%)
    pallas_call x1, Pallas kernels, local(): pl.pallas_call(kernel, out_shape=jax.ShapeDtypeStruct((GROUP, QROWS, HD),...  51.5 us
    unnamed x1, local copies, waits for them, and re-layouts  2.26 us

profile of v4, /device:TPU:252, one launch (start us, length us, event | category | flops | bytes accessed | tf_op | source)
XLA Modules:
  0.0 53.8 jit_solution(6266013824027202041)
XLA Ops:
  0.0 51.5 %sparse_attention.1 = bf16[4,1024,128]{2,1,0:T(8,128)(2,1)} custom-call(s32[1,8]{1,0:T(1,128)} %verts.1, s32[1,4]{1,0:T(1,128)} %slashes.1, bf16[4,1024,128]{2,1,0:T(8,128)(2,1)} %q_hbm.1, bf16[16,128,128]{2,1,0:T(8,128)(2,1)} %bitcast.4, bf16[16,128,128]{2,1,0:T(8,128)(2,1)} %bitcast.5, bf16[8,128,128]{2,1,0:T(8,128)(2,1)} %bitcast.6, ...), custom_call_target="tpu_custom_call" | custom-call | flops 3500000000 | bytes 4000000 | tf_op jit(solution)/shard_map/sparse_attention/pallas_call | solution.py:478
  51.5 2.3 %copy.9 = bf16[4,1024,128]{2,1,0:T(8,128)(2,1)} copy(bf16[4,1024,128]{2,1,0:T(8,128)(2,1)} %sparse_attention.1) | data formatting | bytes 2097152
